TPU v7x, 32 devices: a whole 2x2x4 slice. The times are simulated.
32 devices in a mesh: row: 4 (over z), col: 4 (over y, core), rep: 2 (over x).
Axes of the slice: x: 2, y: 2, z: 4, core: 2. Of those that a mesh axis runs over, the one named last changes fastest.
Arguments:
- hidden: bfloat16 [2, 2048, 2048], P('rep', ('row', 'col')), may hold values from -6 to 6
- lengths: int32 [2, 4], P('rep'), may hold values from 1 to 1536, 2048 in all within a row
- prefix_latent: bfloat16 [512, 576], P(('row', 'col', 'rep')), may hold values from -6 to 6
- gain_in: bfloat16 [2048], replicated, may hold values from 0.25 to 1.75
- query_weight: bfloat16 [2048, 1536], replicated, may hold values from -0.125 to 0.125
- latent_down: bfloat16 [2048, 576], replicated, may hold values from -0.125 to 0.125
- latent_gain: bfloat16 [512], replicated, may hold values from 0.25 to 1.75
- key_absorb: bfloat16 [8, 128, 512], replicated, may hold values from -8 to 8
- value_up: bfloat16 [8, 512, 128], replicated, may hold values from -0.25 to 0.25
- output_weight: bfloat16 [1024, 2048], replicated, may hold values from -0.5 to 0.5
- post_gain: bfloat16 [2048], replicated, may hold values from 0.25 to 1.75
- routes: int32 [2, 2048, 6], P('rep', ('row', 'col')), may hold values from 0 to 63, all different within a row; in each aligned block of 128 rows (0 to 127, 128 to 255, ..., all dimensions but the last counted through in order) at most 16 rows name the same one
- gate_weights: float32 [2, 2048, 6], P('rep', ('row', 'col')), may hold values from 0.1 to 1
- expert_gate_up: bfloat16 [128, 2048, 1408], P(('row', 'col', 'rep')), may hold values from -0.125 to 0.125
- expert_down: bfloat16 [128, 704, 2048], P(('row', 'col', 'rep')), may hold values from -0.15625 to 0.15625
Outputs:
- attended: bfloat16 [2, 2048, 2048], P('rep', ('row', 'col'))
- layer_out: bfloat16 [2, 2048, 2048], P('rep', ('row', 'col'))
Inputs may be any that keep to these rules, and one draw needn't show every extreme that they name: In each group the 4 lengths sum to 2048, and one of them is exactly 1536. `routes`: A token's 6 experts differ; among the 128 tokens of one device (aligned blocks of 128 tokens of a group) no expert is chosen more than 16 times, a bound that some block reaches.
All inputs are finite; a program needn't handle non-finite values.
Results may differ from a plain program's by a relative error of at most 0.014.
The roundings to bfloat16 on the way count: a program that leaves them out, or rounds other values in their place, can miss the bound.
Values may be sent and summed in bfloat16 or wider, within the bound.
A program may use at most 128 MiB of HBM per device.

v0:
```python
import jax
import jax.numpy as jnp
from jax import lax
from jax.sharding import PartitionSpec as P

E = 64
CAP = 16


epsilon = 1e-06
rope_base = 50000.0
floor_value = -1e30


def rms_scale(values, gain_vector):
    mean_square = jnp.mean(values * values, axis=-1, keepdims=True)
    return values * lax.rsqrt(mean_square + epsilon) * gain_vector.astype(jnp.float32)


def rope_tables(positions, rope_width):
    halfway = rope_width // 2
    frequency = jnp.power(rope_base, -2.0 * jnp.arange(halfway, dtype=jnp.float32) / rope_width)
    angles = positions.astype(jnp.float32)[:, None] * frequency[None, :]
    return (jnp.cos(angles), jnp.sin(angles))


def rotate(values, cosine, sine_table):
    halfway = values.shape[-1] // 2
    leading = values[..., :halfway]
    trailing = values[..., halfway:]
    return jnp.concatenate(
        [leading * cosine - trailing * sine_table, trailing * cosine + leading * sine_table],
        axis=-1,
    )


def token_layout(group_lengths, first_place, row_count):
    ends = jnp.cumsum(group_lengths)
    starts = ends - group_lengths
    places = first_place + jnp.arange(row_count, dtype=jnp.int32)
    member = jnp.sum((places[:, None] >= ends[None, :]).astype(jnp.int32), axis=1)
    chosen = member[:, None] == jnp.arange(group_lengths.shape[0], dtype=jnp.int32)[None, :]
    offsets = jnp.sum(jnp.where(chosen, starts[None, :], 0), axis=1)
    return (member, places, places - offsets)


def make_queries(normed, positions, query_weight, latent_down, latent_gain, key_absorb):
    row_count = normed.shape[0]
    head_count = key_absorb.shape[0]
    plain_width = key_absorb.shape[1]
    latent_width = latent_gain.shape[0]
    projected = jnp.dot(normed, query_weight, preferred_element_type=jnp.float32).reshape(
        row_count, head_count, -1
    )
    rope_width = projected.shape[-1] - plain_width
    cosine, sine_table = rope_tables(positions, rope_width)
    query_plain = projected[..., :plain_width].astype(jnp.bfloat16)
    query_rotary = rotate(
        projected[..., plain_width:], cosine[:, None, :], sine_table[:, None, :]
    ).astype(jnp.bfloat16)
    query_latent = jnp.einsum(
        "thn,hnr->thr", query_plain, key_absorb, preferred_element_type=jnp.float32
    ).astype(jnp.bfloat16)
    query_rows = jnp.concatenate([query_latent, query_rotary], axis=-1)
    compressed = jnp.dot(normed, latent_down, preferred_element_type=jnp.float32)
    latent = rms_scale(compressed[:, :latent_width], latent_gain)
    key_rotary = rotate(compressed[:, latent_width:], cosine, sine_table)
    key_rows = jnp.concatenate([latent, key_rotary], axis=-1).astype(jnp.bfloat16)
    return (query_rows, key_rows)


def attend_block(state_now, query_rows, key_block, visible, scale_factor, latent_width):
    running_max, running_sum, weighted_sum = state_now
    scores = (
        lax.dot_general(
            query_rows, key_block, (((1,), (1,)), ((), ())), preferred_element_type=jnp.float32
        )
        * scale_factor
    )
    scores = jnp.where(visible, scores, -jnp.inf)
    new_max = jnp.maximum(running_max, jnp.max(scores, axis=1))
    rescale = jnp.exp(running_max - new_max)
    weights = jnp.exp(scores - new_max[:, None])
    running_sum = running_sum * rescale + jnp.sum(weights, axis=1)
    weighted_sum = weighted_sum * rescale[:, None] + jnp.dot(
        weights.astype(jnp.bfloat16),
        key_block[:, :latent_width],
        preferred_element_type=jnp.float32,
    )
    return (new_max, running_sum, weighted_sum)


def expert_apply(token_rows, expert_gate_up, expert_down):
    hidden_units = expert_down.shape[1]
    joint = jnp.einsum(
        "...hsd,hdf->...hsf", token_rows, expert_gate_up, preferred_element_type=jnp.float32
    )
    active = (jax.nn.silu(joint[..., :hidden_units]) * joint[..., hidden_units:]).astype(
        jnp.bfloat16
    )
    return jnp.einsum(
        "...hsf,hfd->...hsd", active, expert_down, preferred_element_type=jnp.float32
    ).astype(jnp.bfloat16)


def on_device(
    hidden,
    lengths,
    prefix_latent,
    gain_in,
    query_weight,
    latent_down,
    latent_gain,
    key_absorb,
    value_up,
    output_weight,
    post_gain,
    routes,
    gate_weights,
    expert_gate_up,
    expert_down,
):
    token_count = hidden.shape[1]
    model_width = hidden.shape[2]
    head_count = key_absorb.shape[0]
    latent_width = latent_gain.shape[0]
    scale_factor = float(query_weight.shape[1] // head_count) ** (-0.5)
    group_lengths = lengths[0]
    prefix_total = prefix_latent.shape[0] * lax.axis_size(("row", "col", "rep"))
    first_place = lax.axis_index(("row", "col")) * token_count
    member, places, offsets = token_layout(group_lengths, first_place, token_count)
    own_tokens = hidden[0]
    normed = rms_scale(own_tokens.astype(jnp.float32), gain_in).astype(jnp.bfloat16)
    query_rows, key_rows = make_queries(
        normed, prefix_total + offsets, query_weight, latent_down, latent_gain, key_absorb
    )
    query_rows = query_rows.reshape(token_count * head_count, -1)
    row_member = jnp.repeat(member, head_count)
    row_places = jnp.repeat(places, head_count)
    row_total = token_count * head_count
    initial = (
        jnp.full((row_total,), floor_value, jnp.float32),
        jnp.zeros((row_total,), jnp.float32),
        jnp.zeros((row_total, latent_width), jnp.float32),
    )
    after_prefix = attend_block(
        initial,
        query_rows,
        lax.all_gather(prefix_latent, ("row", "col", "rep"), axis=0, tiled=True),
        True,
        scale_factor,
        latent_width,
    )
    key_block = lax.all_gather(key_rows, ("row", "col"), axis=0, tiled=True)
    block_member, block_places, block_offsets = token_layout(
        group_lengths, jnp.int32(0), key_block.shape[0]
    )
    visible = (row_member[:, None] == block_member[None, :]) & (
        row_places[:, None] >= block_places[None, :]
    )
    final_state = attend_block(
        after_prefix, query_rows, key_block, visible, scale_factor, latent_width
    )
    running_max, running_sum, weighted_sum = final_state
    mixed = (
        (weighted_sum / running_sum[:, None])
        .astype(jnp.bfloat16)
        .reshape(token_count, head_count, latent_width)
    )
    head_values = (
        jnp.einsum("thr,hrv->thv", mixed, value_up, preferred_element_type=jnp.float32)
        .astype(jnp.bfloat16)
        .reshape(token_count, -1)
    )
    attention = jnp.dot(head_values, output_weight, preferred_element_type=jnp.float32)
    residual = (own_tokens.astype(jnp.float32) + attention).astype(jnp.bfloat16)
    normed_post = rms_scale(residual.astype(jnp.float32), post_gain).astype(jnp.bfloat16)
    top_count = routes.shape[2]
    choices_flat = routes[0].reshape(-1)
    selected = (choices_flat[:, None] == jnp.arange(E, dtype=jnp.int32)[None, :]).astype(jnp.int32)
    slot_index = jnp.sum(jnp.cumsum(selected, axis=0) * selected, axis=1) - 1
    token_index = jnp.arange(choices_flat.shape[0], dtype=jnp.int32) // top_count
    slot_table = (
        jnp.full((E, CAP), token_count, jnp.int32).at[choices_flat, slot_index].set(token_index)
    )
    padded = jnp.concatenate([normed_post, jnp.zeros((1, model_width), jnp.bfloat16)], axis=0)
    gathered_rows = jnp.take(padded, slot_table.reshape(-1), axis=0).reshape(E, CAP, model_width)
    device_count = lax.axis_size(("row", "col", "rep"))
    per_device = expert_gate_up.shape[0]
    outgoing = jnp.broadcast_to(gathered_rows[:, None], (E, 2, CAP, model_width)).reshape(
        device_count, per_device, CAP, model_width
    )
    produced = expert_apply(
        lax.all_to_all(outgoing, ("row", "col", "rep"), split_axis=0, concat_axis=0, tiled=True),
        expert_gate_up,
        expert_down,
    )
    returned = lax.all_to_all(
        produced, ("row", "col", "rep"), split_axis=0, concat_axis=0, tiled=True
    )
    returned = returned.reshape(E, 2, CAP, model_width)
    paired = returned[:, 0].astype(jnp.float32) + returned[:, 1].astype(jnp.float32)
    picked = jnp.take(
        paired.reshape(E * CAP, model_width), choices_flat * CAP + slot_index, axis=0
    ).reshape(token_count, top_count, model_width)
    mixture = jnp.sum(picked * gate_weights[0][:, :, None], axis=1)
    layer_out = (residual.astype(jnp.float32) + mixture).astype(jnp.bfloat16)
    return (attention.astype(jnp.bfloat16)[None], layer_out[None])


def solution(mesh):
    in_specs = (
        P("rep", ("row", "col"), None),
        P("rep", None),
        P(("row", "col", "rep"), None),
        P(),
        P(),
        P(),
        P(),
        P(),
        P(),
        P(),
        P(),
        P("rep", ("row", "col"), None),
        P("rep", ("row", "col"), None),
        P(("row", "col", "rep"), None, None),
        P(("row", "col", "rep"), None, None),
    )
    out_specs = (P("rep", ("row", "col"), None), P("rep", ("row", "col"), None))
    return jax.shard_map(
        on_device, mesh=mesh, in_specs=in_specs, out_specs=out_specs, check_vma=False
    )
```

profile of v0, /device:TPU:0, one launch (start us, length us, event | category | flops | bytes accessed | tf_op | source)
XLA Modules:
  0.0 638.8 jit_solution(14591191970935330933)
XLA Ops:
  7.3 1.0 reduce-window.10
  9.1 0.7 convert_element_type.107
  9.8 1.2 fusion.34
  11.7 1.9 fusion.52
  15.2 8.7 %copy.77 = bf16[2048,1536]{0,1:T(8,128)(2,1)} copy(bf16[2048,1536]{1,0:T(8,128)(2,1)} %param.19) | data formatting | bytes 12582912 | tf_op args[4]
  24.0 4.8 fusion.50
  29.6 1.8 reduce-window.11
  32.0 37.5 %scatter_fusion = s32[64,16]{0,1:T(8,128)S(1)} fusion(s32[64,16]{0,1:T(8,128)S(1)} %broadcast_in_dim.105, s32[768]{0:T(1024)S(1)} %get-tuple-element.3, s32[768]{0:T(1024)S(1)} %add_select_fusion), kind=kCustom, calls=%fused_computation.2 | custom fusion | bytes 15360 | tf_op jit(solution)/shard_map/scatter | solution.py:184
  69.9 1.7 fusion.24
  71.8 73.4 %all_gather.6 = bf16[512,576]{1,0:T(8,128)(2,1)S(1)} all-gather(bf16[16,576]{1,0:T(8,128)(2,1)S(1)} %copy-done.9), channel_id=1, replica_groups=mesh['row'=4,'col'=4,'rep'=2] {'row','col','rep'}, dimensions={0}, use_global_device_ids=true | all-gather | bytes 608256 | tf_op jit(solution)/shard_map/all_gather | solution.py:149
  145.2 2.6 multiply_reduce_fusion.1
  147.8 6.4 %fusion.73 = (f32[1024]{0:T(1024)S(1)}, f32[1024,2048]{1,0:T(8,128)S(1)}) fusion(bf16[2048,576]{0,1:T(8,128)(2,1)} %all-gather.2.cloned.1.call-done, bf16[128,8,576]{2,0,1:T(8,128)(2,1)} %copy-done.7, s32[1024]{0:T(1024)S(1)} %ge.70, s32[2048]{0:T(1024)S(1)} %convert_reduce_fusion, s32[1024]{0:T(1024)S(1)} %eq.54), kind=kOutput, calls=%fused_computation.136 | convolution fusion | flops 2428500992 | bytes 11948032 | tf_op jit(solution)/shard_map/dot_general | solution.py:75
  154.3 1.3 fusion.6
  156.6 2.4 fusion.16
  159.0 1.6 fusion.25
  160.6 0.9 convolution_convert_fusion.1
  161.5 1.6 fusion.40
  163.1 0.8 copy-done.3
  164.1 6.0 gather_fusion
  170.1 2.6 broadcast_select_fusion
  172.8 4.3 broadcast_in_dim.108
  177.0 187.2 %all_to_all.10 = bf16[32,4,16,2048]{3,2,1,0:T(8,128)(2,1)} all-to-all(bf16[32,4,16,2048]{3,2,1,0:T(8,128)(2,1)} %bitcast.108), channel_id=1, replica_groups=mesh['row'=4,'col'=4,'rep'=2] {'row','col','rep'}, dimensions={0} | all-to-all | bytes 16777216 | tf_op jit(solution)/shard_map/all_to_all | solution.py:194
  364.2 21.2 %fusion.8 = f32[32,4,16,1408]{3,2,0,1:T(8,128)} fusion(bf16[4,2048,1408]{2,1,0:T(8,128)(2,1)} %param.28, bf16[32,4,16,2048]{3,2,1,0:T(8,128)(2,1)} %all_to_all.10), kind=kOutput, calls=%fused_computation.17 | convolution fusion | flops 11811160064 | bytes 42991616 | tf_op jit(solution)/shard_map/...hsd,hdf->...hsf/dot_general | solution.py:95
  385.4 15.5 %convert_bitcast_fusion = bf16[32,4,16,2048]{3,2,0,1:T(8,128)(2,1)} fusion(bf16[4,704,2048]{2,1,0:T(8,128)(2,1)} %param.29, f32[32,4,16,1408]{3,2,0,1:T(8,128)} %fusion.8), kind=kOutput, calls=%fused_computation.10 | convolution fusion | flops 5918425088 | bytes 32505856 | tf_op jit(solution)/shard_map/...hsf,hfd->...hsd/dot_general | solution.py:101
  400.9 8.4 %copy.94 = bf16[32,4,16,2048]{3,2,1,0:T(8,128)(2,1)} copy(bf16[32,4,16,2048]{3,2,0,1:T(8,128)(2,1)} %convert_bitcast_fusion) | data formatting | bytes 16777216 | tf_op jit(solution)/shard_map/convert_element_type | solution.py:103
  409.3 4.1 all-to-all-start.1
  413.9 183.4 %all-to-all-done.1 = bf16[32,4,16,2048]{3,2,1,0:T(8,128)(2,1)} async-done(((bf16[32,4,16,2048]{3,2,1,0:T(8,128)(2,1)}), bf16[32,4,16,2048]{3,2,1,0:T(8,128)(2,1)}, u32[]{:S(2)}, u32[]{:S(2)}) %all-to-all-start.1) | async-done | bytes 8388640 | tf_op jit(solution)/shard_map/all_to_all | solution.py:198
  597.3 8.6 %convert_add_fusion = f32[64,1,16,2048]{3,2,1,0:T(8,128)} fusion(bf16[64,2,16,2048]{3,2,1,0:T(8,128)(2,1)} %bitcast.26), kind=kLoop, calls=%fused_computation.9 | loop fusion | flops 6291456 | bytes 16777216 | tf_op jit(solution)/shard_map/add | solution.py:202
  605.9 10.6 %gather_fusion.1 = f32[768,2048]{1,0:T(8,128)} fusion(f32[1024,2048]{1,0:T(8,128)} %bitcast.107, s32[1024]{0:T(1024)S(1)} %pad_clamp_fusion), kind=kCustom, calls=%fused_computation.1 | custom fusion | bytes 12585984 | tf_op jit(solution)/shard_map/jit(_take)/gather | solution.py:203
  616.5 7.8 %gather.15 = f32[128,6,2048]{2,1,0:T(8,128)} reshape(f32[768,2048]{1,0:T(8,128)} %gather_fusion.1) | data formatting | bytes 12582912 | tf_op jit(solution)/shard_map/jit(_take)/gather | solution.py:203
  624.3 6.7 %multiply_reduce_fusion = f32[128,2048]{1,0:T(8,128)S(1)} fusion(f32[128,6,2048]{2,1,0:T(8,128)} %gather.15, f32[128,6]{1,0:T(8,128)S(1)} %bitcast.112, pred[128,6]{1,0:T(8,128)(4,1)S(1)} %copy.89), kind=kLoop, calls=%fused_computation.8 | loop fusion | flops 4456448 | bytes 7343872 | tf_op jit(solution)/shard_map/reduce_sum | solution.py:206
  631.0 0.9 fusion.48
  (83 shorter events, 6.8 us)
Async XLA Ops:
  7.2 4.5 copy-start
  7.2 7.5 %copy-start.10 = (s32[1,128,6]{1,0,2:T(1,128)S(1)}, s32[1,128,6]{1,0,2:T(1,128)}, u32[]{:S(2)}) copy-start(s32[1,128,6]{1,0,2:T(1,128)} %param.26) | copy-start | bytes 9220
  7.2 140.6 %all-gather.2.cloned.1.call-start = ((), (), s32[]{:S(2)}) async-start(), calls=%async_computation.2 | async-start | bytes 2506752 | tf_op jit(solution)/shard_map/all_gather | solution.py:154
  15.2 8.8 %copy-start.2 = (bf16[1,128,2048]{2,1,0:T(8,128)(2,1)S(1)}, bf16[1,128,2048]{2,1,0:T(8,128)(2,1)}, u32[]{:S(2)}) copy-start(bf16[1,128,2048]{2,1,0:T(8,128)(2,1)} %param.15) | copy-start | bytes 1572868
  24.0 5.6 copy-start.11
  69.5 2.4 copy-start.9
  71.8 73.4 %copy-start.7 = (bf16[128,8,576]{2,0,1:T(8,128)(2,1)}, bf16[128,8,576]{2,0,1:T(8,128)(2,1)S(1)}, u32[]{:S(2)}) copy-start(bf16[128,8,576]{2,0,1:T(8,128)(2,1)S(1)} %pad_maximum_fusion) | copy-start | bytes 3538948
  154.3 1.6 copy-start.6
  154.3 2.3 copy-start.13
  159.0 1.6 copy-start.8
  159.0 2.5 copy-start.5
  163.1 0.8 copy-start.3
  409.3 4.2 copy-start.12
  409.3 187.9 %all-to-all-start.1 = ((bf16[32,4,16,2048]{3,2,1,0:T(8,128)(2,1)}), bf16[32,4,16,2048]{3,2,1,0:T(8,128)(2,1)}, u32[]{:S(2)}, u32[]{:S(2)}) async-start(bf16[32,4,16,2048]{3,2,1,0:T(8,128)(2,1)} %copy.94), calls=%async_computation.1 | async-start | bytes 16777216 | tf_op jit(solution)/shard_map/all_to_all | solution.py:198
  624.3 7.6 %copy-start.1 = (bf16[2048,576]{0,1:T(8,128)(2,1)S(1)}, bf16[2048,576]{0,1:T(8,128)(2,1)}, u32[]{:S(2)}) copy-start(bf16[2048,576]{0,1:T(8,128)(2,1)} %param.20) | copy-start | bytes 7077892
  624.3 6.7 %copy-start.4 = (bf16[128,2048]{1,0:T(8,128)(2,1)S(1)}, bf16[128,2048]{1,0:T(8,128)(2,1)}, u32[]{:S(2)}) copy-start(bf16[128,2048]{1,0:T(8,128)(2,1)} %copy-done.3) | copy-start | bytes 1572868
Sparse Core Ops, SparseCore 0:
  14.8 45.3 all-gather.1
where the time goes:
time: 640 us; the launch traced here: 639 us
  blocking collectives  261 us (41%)
  waiting for transfers between devices  183 us (29%)
  local copies, waits for them, and re-layouts  87.2 us (14%)
  matrix products  60.5 us (9%)
  other arithmetic  28.6 us (4%)
  between operations  14.4 us (2%)
    all_to_all x1, blocking collectives, on_device(): lax.all_to_all(outgoing, ('row', 'col', 'rep'), split_axis=0, concat_axis...  187 us
    all_to_all x1, waiting for transfers between devices, on_device(): lax.all_to_all(produced, ('row', 'col', 'rep'), split_axis=0, concat_axis...  183 us
    all_gather x1, blocking collectives, on_device(): lax.all_gather(prefix_latent, ('row', 'col', 'rep'), axis=0, tiled=True)  73.4 us
    scatter x2, local copies, waits for them, and re-layouts, on_device(): jnp.full((E, CAP), token_count, jnp.int32).at[choices_flat, slot_index]  37.6 us
    dot_general x1, matrix products, expert_apply(): jnp.einsum('...hsd,hdf->...hsf', token_rows, expert_gate_up, preferred_el...  21.2 us
    gather x2, local copies, waits for them, and re-layouts, on_device(): jnp.take(paired.reshape(E * CAP, model_width), choices_flat * CAP + slot_...  18.4 us
    dot_general x1, matrix products, expert_apply(): jnp.einsum('...hsf,hfd->...hsd', active, expert_down, preferred_element_t...  15.5 us
  transfers between devices with their start and end apart: 2, of which 1 were waited for; matrix products, arithmetic and copies ran while one was open for 9% of the time, Pallas kernels for 0%

commit v1 on v0

v1 whole, which is shorter than its diff:
```python
import jax
import jax.numpy as jnp
import functools
from jax import lax
from jax.experimental import pallas as pl
from jax.experimental.pallas import tpu as pltpu
from jax.sharding import PartitionSpec as P

E = 64
CAP = 16


epsilon = 1e-06
rope_base = 50000.0


def rms_scale(values, gain_vector):
    mean_square = jnp.mean(values * values, axis=-1, keepdims=True)
    return values * lax.rsqrt(mean_square + epsilon) * gain_vector.astype(jnp.float32)


def rope_tables(positions, rope_width):
    halfway = rope_width // 2
    frequency = jnp.power(rope_base, -2.0 * jnp.arange(halfway, dtype=jnp.float32) / rope_width)
    angles = positions.astype(jnp.float32)[:, None] * frequency[None, :]
    return (jnp.cos(angles), jnp.sin(angles))


def rotate(values, cosine, sine_table):
    halfway = values.shape[-1] // 2
    leading = values[..., :halfway]
    trailing = values[..., halfway:]
    return jnp.concatenate(
        [leading * cosine - trailing * sine_table, trailing * cosine + leading * sine_table],
        axis=-1,
    )


def make_queries(normed, positions, query_weight, latent_down, latent_gain, key_absorb):
    row_count = normed.shape[0]
    head_count = key_absorb.shape[0]
    plain_width = key_absorb.shape[1]
    latent_width = latent_gain.shape[0]
    projected = jnp.dot(normed, query_weight, preferred_element_type=jnp.float32).reshape(
        row_count, head_count, -1
    )
    rope_width = projected.shape[-1] - plain_width
    cosine, sine_table = rope_tables(positions, rope_width)
    query_plain = projected[..., :plain_width].astype(jnp.bfloat16)
    query_rotary = rotate(
        projected[..., plain_width:], cosine[:, None, :], sine_table[:, None, :]
    ).astype(jnp.bfloat16)
    query_latent = jnp.einsum(
        "thn,hnr->thr", query_plain, key_absorb, preferred_element_type=jnp.float32
    ).astype(jnp.bfloat16)
    query_rows = jnp.concatenate([query_latent, query_rotary], axis=-1)
    compressed = jnp.dot(normed, latent_down, preferred_element_type=jnp.float32)
    latent = rms_scale(compressed[:, :latent_width], latent_gain)
    key_rotary = rotate(compressed[:, latent_width:], cosine, sine_table)
    key_rows = jnp.concatenate([latent, key_rotary], axis=-1).astype(jnp.bfloat16)
    return (query_rows, key_rows)


MESH = pl.DeviceIdType.MESH
VMEM_BYTES = 48 * 1024 * 1024


def position():
    return lax.axis_index("row"), lax.axis_index("col"), lax.axis_index("rep")


def greet(peers):
    barrier = pltpu.get_barrier_semaphore()
    for peer in peers:
        pl.semaphore_signal(barrier, inc=1, device_id=peer, device_id_type=MESH)
    pl.semaphore_wait(barrier, len(peers))


def remote(source, target, send, recv, peer):
    return pltpu.make_async_remote_copy(
        src_ref=source,
        dst_ref=target,
        send_sem=send,
        recv_sem=recv,
        device_id=peer,
        device_id_type=MESH,
    )


def gather_kernel(sizes, kv_ref, prefix_ref, out_ref, local, rep_sems, row_sems, col_sems):
    rows, cols, reps = sizes
    row, col, rep = position()
    tokens, shard = kv_ref.shape[0], prefix_ref.shape[0]
    strides = []
    stride = cols // 2
    while stride:
        strides.append(stride)
        stride //= 2

    def across(index, stride):
        return index + stride * (1 - 2 * (lax.div(index, stride) % 2))

    rep_peers = [(row, col, lax.rem(rep + d, reps)) for d in range(1, reps)]
    row_peers = [(lax.rem(row + d, rows), col, rep) for d in range(1, rows)]
    col_peers = [(row, across(col, s), rep) for s in strides]
    greet(rep_peers + row_peers + col_peers)
    mine = out_ref.at[row, col, pl.ds(tokens + rep * shard, shard)]
    pending = []
    keep = [
        pltpu.make_async_copy(kv_ref, out_ref.at[row, col, pl.ds(0, tokens)], local.at[0]),
        pltpu.make_async_copy(prefix_ref, mine, local.at[1]),
    ]
    early = [
        remote(prefix_ref, mine, rep_sems.at[0, d], rep_sems.at[1, d], peer)
        for d, peer in enumerate(rep_peers)
    ]
    for copy in early + keep:
        copy.start()
    for copy in keep:
        copy.wait()
    for copy in early:
        copy.wait()
    own = out_ref.at[row, col]
    arrivals = [None]
    for d, peer in enumerate(row_peers):
        copy = remote(own, own, row_sems.at[0, d], row_sems.at[1, d], peer)
        copy.start()
        arrivals.append(copy)
    sent = {}

    def forward(step, d, m, held_col):
        block = out_ref.at[lax.rem(row + rows - d, rows), held_col]
        copy = remote(
            block, block, col_sems.at[0, step, d, m], col_sems.at[1, step, d, m], col_peers[step]
        )
        copy.start()
        sent[step, d, m] = copy

    for d in range(rows):
        if d:
            arrivals[d].wait_recv()
        for step in range(len(strides)):
            forward(step, d, 0, col)
    held = [col]
    for step, stride in enumerate(strides):
        fresh = [across(c, stride) for c in held]
        for d in range(rows):
            for m, c in enumerate(fresh):
                sent[step, d, m].wait_recv()
                for later in range(step + 1, len(strides)):
                    forward(later, d, len(held) + m, c)
        held = held + fresh
    for copy in arrivals[1:]:
        copy.wait_send()
    for copy in sent.values():
        copy.wait_send()


def gather_keys(key_rows, prefix_latent):
    rows, cols, reps = (lax.axis_size(name) for name in ("row", "col", "rep"))
    shard, width = prefix_latent.shape
    steps = max(1, cols.bit_length() - 1)
    return pl.pallas_call(
        functools.partial(gather_kernel, (rows, cols, reps)),
        out_shape=jax.ShapeDtypeStruct(
            (rows, cols, key_rows.shape[0] + reps * shard, width), jnp.bfloat16
        ),
        in_specs=[pl.BlockSpec(memory_space=pltpu.VMEM)] * 2,
        out_specs=pl.BlockSpec(memory_space=pl.ANY),
        scratch_shapes=[
            pltpu.SemaphoreType.DMA((2,)),
            pltpu.SemaphoreType.DMA((2, reps)),
            pltpu.SemaphoreType.DMA((2, rows)),
            pltpu.SemaphoreType.DMA((2, steps, rows, cols)),
        ],
        compiler_params=pltpu.CompilerParams(collective_id=0, has_side_effects=True),
    )(key_rows, prefix_latent)


def plane_peers(sizes):
    rows, cols, reps = sizes
    row, col, rep = position()
    plane = cols * reps
    me = col * reps + rep
    others = [lax.rem(me + k, plane) for k in range(1, plane)]
    peers = [(row, lax.div(q, reps), lax.rem(q, reps)) for q in others]
    down = [(lax.rem(row + d, rows), col, rep) for d in range(1, rows)]
    return row, me, others, peers, down


def turns(rows):
    return sorted(range(rows), key=lambda d: (min(d, rows - d), d))


def dispatch_kernel(
    sizes, x_ref, tab_ref, out_ref, tabs_ref, xbuf, tbuf, rbuf, local, xsem, tsem, psem
):
    rows, cols, reps = sizes
    row, me, others, peers, down = plane_peers(sizes)
    tokens, width = x_ref.shape
    held = out_ref.shape[0]
    slots = tab_ref.shape[2]
    greet(peers + down)
    streams = [None]
    for d in range(1, rows):
        peer = down[d - 1]
        table = remote(tab_ref.at[peer[0]], tbuf.at[d], tsem.at[0, d], tsem.at[1, d], peer)
        block = remote(x_ref, xbuf.at[d], xsem.at[0, d], xsem.at[1, d], peer)
        table.start()
        block.start()
        streams.append((table, block))
    tabs_ref[0] = tab_ref[row]
    place = lax.broadcasted_iota(jnp.int32, (tokens, slots), 0).astype(jnp.float32)
    tile = min(width, 512)
    waiting = []
    for d in turns(rows):
        if d:
            streams[d][0].wait_recv()
            streams[d][1].wait_recv()
            tabs_ref[d] = tbuf[d]
        table = tabs_ref[d]
        onehot = jnp.where(place == table[0:1, :], 1.0, 0.0).astype(jnp.bfloat16)
        for start in range(0, width, tile):
            part = x_ref[:, start : start + tile] if d == 0 else xbuf[d, :, start : start + tile]
            picked = lax.dot_general(
                onehot, part, (((0,), (0,)), ((), ())), preferred_element_type=jnp.float32
            ).astype(jnp.bfloat16)
            rbuf[d, :, :, :, start : start + tile] = picked.reshape(-1, held, CAP, tile)
        origin = lax.rem(row + rows - d, rows)
        target = out_ref.at[:, origin, me]
        for k, (q, peer) in enumerate(zip(others, peers)):
            copy = remote(rbuf.at[d, q], target, psem.at[0, d, k], psem.at[1, d, k], peer)
            copy.start()
            waiting.append(copy)
        copy = pltpu.make_async_copy(rbuf.at[d, me], target, local.at[d])
        copy.start()
        waiting.append(copy)
    for d in range(1, rows):
        streams[d][0].wait_send()
        streams[d][1].wait_send()
    for copy in waiting:
        copy.wait()


def dispatch(normed, tables, per_device):
    rows, cols, reps = (lax.axis_size(name) for name in ("row", "col", "rep"))
    tokens, width = normed.shape
    slots = tables.shape[2]
    plane = cols * reps
    held = max(1, per_device // 2)
    vmem = pl.BlockSpec(memory_space=pltpu.VMEM)
    return pl.pallas_call(
        functools.partial(dispatch_kernel, (rows, cols, reps)),
        out_shape=(
            jax.ShapeDtypeStruct((held, rows, plane, CAP, width), jnp.bfloat16),
            jax.ShapeDtypeStruct(tables.shape, jnp.float32),
        ),
        in_specs=[vmem, vmem],
        out_specs=(pl.BlockSpec(memory_space=pl.ANY), vmem),
        scratch_shapes=[
            pltpu.VMEM((rows, tokens, width), jnp.bfloat16),
            pltpu.VMEM((rows, 8, slots), jnp.float32),
            pltpu.VMEM((rows, plane, held, CAP, width), jnp.bfloat16),
            pltpu.SemaphoreType.DMA((rows,)),
            pltpu.SemaphoreType.DMA((2, rows)),
            pltpu.SemaphoreType.DMA((2, rows)),
            pltpu.SemaphoreType.DMA((2, rows, plane)),
        ],
        compiler_params=pltpu.CompilerParams(
            collective_id=1, has_side_effects=True, vmem_limit_bytes=VMEM_BYTES
        ),
    )(normed, tables)


def combine_kernel(
    sizes, y_ref, tabs_ref, residual_ref, out_ref, ybuf, sums, pbuf, total, local, psem, rsem
):
    rows, cols, reps = sizes
    row, me, others, peers, down = plane_peers(sizes)
    tokens, width = residual_ref.shape
    slots = tabs_ref.shape[2]
    greet(peers + down)
    order = turns(rows)[::-1]
    waiting = {}
    for d in order:
        origin = lax.rem(row + rows - d, rows)
        waiting[d] = []
        for k, (q, peer) in enumerate(zip(others, peers)):
            copy = remote(
                y_ref.at[:, origin, q], ybuf.at[d, me], psem.at[0, d, k], psem.at[1, d, k], peer
            )
            copy.start()
            waiting[d].append(copy)
        copy = pltpu.make_async_copy(y_ref.at[:, origin, me], ybuf.at[d, me], local.at[d])
        copy.start()
        waiting[d].append(copy)
    place = lax.broadcasted_iota(jnp.int32, (tokens, slots), 0).astype(jnp.float32)
    tile = min(width, 512)
    back = []
    for d in order:
        for copy in waiting[d]:
            copy.wait()
        table = tabs_ref[d]
        gates = jnp.where(place == table[0:1, :], table[1:2, :], 0.0)
        coarse = gates.astype(jnp.bfloat16)
        fine = (gates - coarse.astype(jnp.float32)).astype(jnp.bfloat16)
        for start in range(0, width, tile):
            part = ybuf[d, :, :, :, start : start + tile].reshape(slots, tile)
            mixture = jnp.dot(coarse, part, preferred_element_type=jnp.float32) + jnp.dot(
                fine, part, preferred_element_type=jnp.float32
            )
            if d == 0:
                total[:, start : start + tile] = mixture
            else:
                sums[d, :, start : start + tile] = mixture.astype(jnp.bfloat16)
        if d:
            copy = remote(
                sums.at[d], pbuf.at[d], rsem.at[0, d], rsem.at[1, d], down[rows - d - 1]
            )
            copy.start()
            back.append((d, copy))
    for d, copy in back:
        copy.wait()
        total[...] += pbuf[d].astype(jnp.float32)
    out_ref[...] = (residual_ref[...].astype(jnp.float32) + total[...]).astype(jnp.bfloat16)


def combine(produced, tables, residual):
    rows, cols, reps = (lax.axis_size(name) for name in ("row", "col", "rep"))
    tokens, width = residual.shape
    held, plane = produced.shape[0], cols * reps
    vmem = pl.BlockSpec(memory_space=pltpu.VMEM)
    return pl.pallas_call(
        functools.partial(combine_kernel, (rows, cols, reps)),
        out_shape=jax.ShapeDtypeStruct((tokens, width), jnp.bfloat16),
        in_specs=[pl.BlockSpec(memory_space=pl.ANY), vmem, vmem],
        out_specs=vmem,
        scratch_shapes=[
            pltpu.VMEM((rows, plane, held, CAP, width), jnp.bfloat16),
            pltpu.VMEM((rows, tokens, width), jnp.bfloat16),
            pltpu.VMEM((rows, tokens, width), jnp.bfloat16),
            pltpu.VMEM((tokens, width), jnp.float32),
            pltpu.SemaphoreType.DMA((rows,)),
            pltpu.SemaphoreType.DMA((2, rows, plane)),
            pltpu.SemaphoreType.DMA((2, rows)),
        ],
        compiler_params=pltpu.CompilerParams(
            collective_id=2, has_side_effects=True, vmem_limit_bytes=VMEM_BYTES
        ),
    )(produced, tables, residual)


def token_layout(group_lengths, places):
    upto = jnp.tril(jnp.ones((group_lengths.shape[0],) * 2, jnp.int32))
    ends = jnp.sum(upto * group_lengths[None, :], axis=1)
    starts = ends - group_lengths
    member = jnp.sum((places[:, None] >= ends[None, :]).astype(jnp.int32), axis=1)
    chosen = member[:, None] == jnp.arange(group_lengths.shape[0], dtype=jnp.int32)[None, :]
    return member, places - jnp.sum(jnp.where(chosen, starts[None, :], 0), axis=1)


def slot_tables(routes, gates, planes, plane_size, per_device):
    token_count = routes.shape[0]
    experts = jnp.arange(E, dtype=jnp.int32)
    named = routes[:, :, None] == experts[None, None, :]
    chosen = jnp.sum(named.astype(jnp.float32), axis=1)
    gate = jnp.sum(jnp.where(named, gates[:, :, None], 0.0), axis=1)
    before = jnp.tril(jnp.ones((token_count, token_count), jnp.float32), -1)
    rank = jnp.dot(
        before.astype(jnp.bfloat16), chosen.astype(jnp.bfloat16), preferred_element_type=jnp.float32
    )
    slots = jnp.arange(CAP, dtype=jnp.float32)
    filled = (chosen[:, :, None] > 0) & (rank[:, :, None] == slots[None, None, :])
    tokens = jnp.arange(1, token_count + 1, dtype=jnp.float32)
    token = jnp.sum(jnp.where(filled, tokens[:, None, None], 0.0), axis=0) - 1.0
    weight = jnp.sum(jnp.where(filled, gate[:, :, None], 0.0), axis=0)
    held = max(1, per_device // 2)
    both = jnp.stack([token, weight])
    if per_device == 1:
        both = jnp.repeat(both, 2, axis=1)
    both = both.reshape(2, planes, plane_size * held * CAP).swapaxes(0, 1)
    return jnp.concatenate([both, jnp.zeros((planes, 6, both.shape[2]), jnp.float32)], axis=1)


def run_experts(rows, expert_gate_up, expert_down):
    hidden_units = expert_down.shape[1]
    outputs = []
    for half in range(expert_down.shape[0]):
        joint = jnp.dot(
            rows[half // 2], expert_gate_up[half], preferred_element_type=jnp.float32
        )
        active = (jax.nn.silu(joint[:, :hidden_units]) * joint[:, hidden_units:]).astype(
            jnp.bfloat16
        )
        outputs.append(
            jnp.dot(active, expert_down[half], preferred_element_type=jnp.float32)
            .astype(jnp.bfloat16)
            .astype(jnp.float32)
        )
    if len(outputs) == 1:
        return outputs[0][None].astype(jnp.bfloat16)
    return jnp.stack(
        [(outputs[i] + outputs[i + 1]).astype(jnp.bfloat16) for i in range(0, len(outputs), 2)]
    )


def on_device(
    hidden,
    lengths,
    prefix_latent,
    gain_in,
    query_weight,
    latent_down,
    latent_gain,
    key_absorb,
    value_up,
    output_weight,
    post_gain,
    routes,
    gate_weights,
    expert_gate_up,
    expert_down,
):
    token_count = hidden.shape[1]
    head_count = key_absorb.shape[0]
    latent_width = latent_gain.shape[0]
    scale_factor = float(query_weight.shape[1] // head_count) ** (-0.5)
    group_lengths = lengths[0]
    rows, cols, reps = (lax.axis_size(name) for name in ("row", "col", "rep"))
    prefix_total = prefix_latent.shape[0] * rows * cols * reps
    places = lax.axis_index(("row", "col")) * token_count + jnp.arange(token_count, dtype=jnp.int32)
    member, offsets = token_layout(group_lengths, places)
    own_tokens = hidden[0]
    normed = rms_scale(own_tokens.astype(jnp.float32), gain_in).astype(jnp.bfloat16)
    query_rows, key_rows = make_queries(
        normed, prefix_total + offsets, query_weight, latent_down, latent_gain, key_absorb
    )
    tables = slot_tables(
        routes[0], gate_weights[0], rows, cols * reps, expert_gate_up.shape[0]
    )
    query_rows = query_rows.reshape(token_count * head_count, -1)
    row_member = jnp.repeat(member, head_count)
    row_places = jnp.repeat(places, head_count)
    keys = gather_keys(key_rows, prefix_latent)
    block_rows = keys.shape[2]
    within = jnp.tile(jnp.arange(block_rows, dtype=jnp.int32), rows * cols)
    key_places = (
        jnp.repeat(jnp.arange(rows * cols, dtype=jnp.int32) * token_count, block_rows) + within
    )
    key_member, _ = token_layout(group_lengths, key_places)
    is_prefix = within >= token_count
    keys = keys.reshape(rows * cols * block_rows, -1)
    visible = is_prefix[None, :] | (
        (row_member[:, None] == key_member[None, :])
        & (row_places[:, None] >= key_places[None, :])
    )
    scores = (
        lax.dot_general(
            query_rows, keys, (((1,), (1,)), ((), ())), preferred_element_type=jnp.float32
        )
        * scale_factor
    )
    scores = jnp.where(visible, scores, -jnp.inf)
    weights = jnp.exp(scores - jnp.max(scores, axis=1, keepdims=True))
    normalizer = jnp.sum(weights, axis=1, keepdims=True)
    weighted = jnp.dot(
        weights.astype(jnp.bfloat16), keys[:, :latent_width], preferred_element_type=jnp.float32
    )
    mixed = (
        (weighted / normalizer).astype(jnp.bfloat16).reshape(token_count, head_count, latent_width)
    )
    head_values = (
        jnp.einsum("thr,hrv->thv", mixed, value_up, preferred_element_type=jnp.float32)
        .astype(jnp.bfloat16)
        .reshape(token_count, -1)
    )
    attention = jnp.dot(head_values, output_weight, preferred_element_type=jnp.float32)
    residual = (own_tokens.astype(jnp.float32) + attention).astype(jnp.bfloat16)
    normed_post = rms_scale(residual.astype(jnp.float32), post_gain).astype(jnp.bfloat16)
    arrived, arrived_tables = dispatch(normed_post, tables, expert_gate_up.shape[0])
    shape = arrived.shape
    produced = run_experts(
        arrived.reshape(shape[0], -1, shape[-1]), expert_gate_up, expert_down
    ).reshape(shape)
    layer_out = combine(produced, arrived_tables, residual)
    return (attention.astype(jnp.bfloat16)[None], layer_out[None])


def solution(mesh):
    in_specs = (
        P("rep", ("row", "col"), None),
        P("rep", None),
        P(("row", "col", "rep"), None),
        P(),
        P(),
        P(),
        P(),
        P(),
        P(),
        P(),
        P(),
        P("rep", ("row", "col"), None),
        P("rep", ("row", "col"), None),
        P(("row", "col", "rep"), None, None),
        P(("row", "col", "rep"), None, None),
    )
    out_specs = (P("rep", ("row", "col"), None), P("rep", ("row", "col"), None))
    return jax.shard_map(
        on_device, mesh=mesh, in_specs=in_specs, out_specs=out_specs, check_vma=False
    )
```

time: 640 us -> 251 us (0.39)
  blocking collectives: 261 us -> 0 us
  waiting for transfers between devices: 183 us -> 0 us
  Pallas kernels: 0 us -> 176 us
  local copies, waits for them, and re-layouts: 87.2 us -> 11.7 us
  other arithmetic: 28.6 us -> 9.07 us
  between operations: 14.4 us -> 1.11 us
  matrix products: 60.5 us -> 52.5 us
    all_to_all x1 -> x0, blocking collectives: 187 us -> none  [on_device(): lax.all_to_all(outgoing, ('row', 'col', 'rep'), split_axis=0, concat_axis...]
    all_to_all x1 -> x0, waiting for transfers between devices: 183 us -> none  [on_device(): lax.all_to_all(produced, ('row', 'col', 'rep'), split_axis=0, concat_axis...]
    pallas_call x0 -> x3, Pallas kernels: none -> 176 us  [the longest x1 83.9 us: combine(): pl.pallas_call(functools.partial(combine_kernel, (rows, cols, reps)), out...]
    all_gather x1 -> x0, blocking collectives: 73.4 us -> none  [on_device(): lax.all_gather(prefix_latent, ('row', 'col', 'rep'), axis=0, tiled=True)]
    scatter x2 -> x0, local copies, waits for them, and re-layouts: 37.6 us -> none  [on_device(): jnp.full((E, CAP), token_count, jnp.int32).at[choices_flat, slot_index]]
    gather x3 -> x0, local copies, waits for them, and re-layouts: 24.4 us -> none  [the longest x2 18.4 us: on_device(): jnp.take(paired.reshape(E * CAP, model_width), choices_flat * CAP + slot_...]
    add x4, other arithmetic: 8.63 us -> 0.09 us  [the longest x1 0.07 us: on_device(): jnp.repeat(jnp.arange(rows * cols, dtype=jnp.int32) * token_count, block_...]
    convert_element_type x1 -> x0, local copies, waits for them, and re-layouts: 8.44 us -> none  [expert_apply(): return jnp.einsum('...hsf,hfd->...hsd', active, expert_down, preferred_el...]
  transfers between devices with their start and end apart: 2 -> 0, of which waited for: 1 -> 0; matrix products, arithmetic and copies ran while one was open for 9% -> 0% of each run, Pallas kernels for 0% -> 0%
where the time goes in v1:
time: 251 us; the launch traced here: 250 us
  Pallas kernels  176 us (70%)
  matrix products  52.5 us (21%)
  local copies, waits for them, and re-layouts  11.7 us (5%)
  other arithmetic  9.07 us (4%)
    pallas_call x1, Pallas kernels, combine(): pl.pallas_call(functools.partial(combine_kernel, (rows, cols, reps)), out...  83.9 us
    pallas_call x1, Pallas kernels, dispatch(): pl.pallas_call(functools.partial(dispatch_kernel, (rows, cols, reps)), ou...  56.1 us
    pallas_call x1, Pallas kernels, gather_keys(): pl.pallas_call(functools.partial(gather_kernel, (rows, cols, reps)), out_...  36.1 us
    dot_general x4, matrix products, run_experts(): jnp.dot(rows[half // 2], expert_gate_up[half], preferred_element_type=jnp...  23.4 us
    unnamed x32, local copies, waits for them, and re-layouts  10 us
    dot_general x4, matrix products, run_experts(): jnp.dot(active, expert_down[half], preferred_element_type=jnp.float32)  7.43 us
    dot_general x1, matrix products, on_device(): lax.dot_general(query_rows, keys, (((1,), (1,)), ((), ())), preferred_ele...  7.38 us

profile of v1, /device:TPU:0, one launch (start us, length us, event | category | flops | bytes accessed | tf_op | source)
XLA Modules:
  0.0 250.4 jit_solution(2186479137349289496)
XLA Ops:
  0.7 0.9 multiply_reduce_fusion.1
  1.7 0.7 fusion.82
  2.4 0.7 convert_element_type.129
  3.1 1.2 fusion.49
  4.4 2.0 fusion.70
  6.4 0.3 multiply_cosine_fusion
  6.8 8.8 %copy.62 = bf16[2048,1536]{0,1:T(8,128)(2,1)} copy(bf16[2048,1536]{1,0:T(8,128)(2,1)} %param.19) | data formatting | bytes 12582912 | tf_op args[4]
  15.6 4.7 %fusion.68 = f32[128,8,192]{0,2,1:T(8,128)S(1)} fusion(bf16[8,192,2048]{2,1,0:T(8,128)(2,1)} %bitcast.100, bf16[1,128,2048]{2,1,0:T(8,128)(2,1)S(1)} %copy-done.2, f32[2048]{0:T(1024)S(1)} %convert_element_type.129, f32[128]{0:T(128)S(1)} %add_rsqrt_fusion.2), kind=kOutput, calls=%fused_computation.72 | convolution fusion | flops 806354944 | bytes 7610880 | tf_op jit(solution)/shard_map/dot_general | solution.py:44
  20.7 1.7 fusion.38
  22.4 1.3 pad_maximum_fusion.1
  23.9 0.8 pad_maximum_fusion.2.kv_ref
  24.7 36.1 %shard_map.158 = bf16[4,4,160,576]{3,2,1,0:T(8,128)(2,1)} custom-call(bf16[128,576]{1,0:T(8,128)(2,1)} %pad_maximum_fusion.2.kv_ref, bf16[16,576]{1,0:T(8,128)(2,1)} %prefix_ref.1), custom_call_target="tpu_custom_call" | custom-call | tf_op jit(solution)/shard_map/pallas_call | solution.py:163
  61.6 7.4 %fusion.91 = (f32[1024]{0:T(1024)S(1)}, f32[1024,2560]{1,0:T(8,128)S(1)}) fusion(bf16[2560,576]{1,0:T(8,128)(2,1)} %bitcast.101, bf16[128,8,576]{2,0,1:T(8,128)(2,1)S(1)} %copy-done.5, s32[2560]{0:T(1024)S(1)} %add.131, s32[1024]{0:T(1024)S(1)} %ge.73, s32[2560]{0:T(1024)S(1)} %convert_reduce_fusion.1, s32[1024]{0:T(1024)S(1)} %eq.56, ...), kind=kOutput, calls=%fused_computation.134 | convolution fusion | flops 3038247936 | bytes 14649856 | tf_op jit(solution)/shard_map/dot_general | solution.py:458
  68.9 1.6 fusion
  70.5 0.4 copy-done.4
  70.9 3.2 %fusion.39 = bf16[128,8,512]{2,1,0:T(8,128)(2,1)S(1)} fusion(bf16[2560,576]{1,0:T(8,128)(2,1)S(1)} %bitcast.102, f32[1024,2560]{1,0:T(8,128)S(1)} %get-tuple-element.24, f32[1024]{0:T(1024)S(1)} %get-tuple-element.23, f32[1024]{0:T(1024)S(1)} %fusion), kind=kOutput, calls=%fused_computation.45 | convolution fusion | flops 2690646016 | bytes 14163968 | tf_op jit(solution)/shard_map/dot_general | solution.py:466
  74.1 0.9 convolution_convert_fusion.5
  75.0 1.6 fusion.55
  77.1 0.4 select_reduce_fusion.1
  77.7 56.1 %shard_map.159 = (bf16[2,4,8,16,2048]{4,3,2,1,0:T(8,128)(2,1)S(1)}, f32[4,8,256]{2,1,0:T(8,128)S(1)}) custom-call(bf16[128,2048]{1,0:T(8,128)(2,1)S(1)} %fusion.57.x_ref, f32[4,8,256]{2,1,0:T(8,128)S(1)} %concatenate.17.tab_ref), custom_call_target="tpu_custom_call" | custom-call | tf_op jit(solution)/shard_map/pallas_call | solution.py:252
  133.8 0.6 fusion.90
  134.4 6.0 %fusion.6 = f32[512,1408]{1,0:T(8,128)S(1)} fusion(bf16[512,2048]{1,0:T(8,128)(2,1)S(1)} %bitcast.106, bf16[4,2048,1408]{2,1,0:T(8,128)(2,1)} %param.28), kind=kOutput, calls=%fused_computation.8 | convolution fusion | flops 2952790016 | bytes 10747904 | tf_op jit(solution)/shard_map/dot_general | solution.py:389
  140.5 1.9 convolution_convert_fusion.2
  142.3 5.7 %fusion.8 = f32[512,1408]{1,0:T(8,128)S(1)} fusion(bf16[512,2048]{1,0:T(8,128)(2,1)S(1)} %bitcast.107, bf16[4,2048,1408]{2,1,0:T(8,128)(2,1)} %param.28), kind=kOutput, calls=%fused_computation.10 | convolution fusion | flops 2952790016 | bytes 10747904 | tf_op jit(solution)/shard_map/dot_general | solution.py:389
  148.1 1.9 add_convert_fusion.1
  149.9 6.0 %fusion.2 = f32[512,1408]{1,0:T(8,128)S(1)} fusion(bf16[512,2048]{1,0:T(8,128)(2,1)S(1)} %bitcast.103, bf16[4,2048,1408]{2,1,0:T(8,128)(2,1)} %param.28), kind=kOutput, calls=%fused_computation.4 | convolution fusion | flops 2952790016 | bytes 10747904 | tf_op jit(solution)/shard_map/dot_general | solution.py:389
  155.9 1.9 convolution_convert_fusion
  157.8 5.7 %fusion.4 = f32[512,1408]{1,0:T(8,128)S(1)} fusion(bf16[512,2048]{1,0:T(8,128)(2,1)S(1)} %bitcast.104, bf16[4,2048,1408]{2,1,0:T(8,128)(2,1)} %param.28), kind=kOutput, calls=%fused_computation.6 | convolution fusion | flops 2952790016 | bytes 10747904 | tf_op jit(solution)/shard_map/dot_general | solution.py:389
  163.5 1.9 add_convert_fusion
  165.4 0.4 pad_maximum_fusion.y_ref
  165.8 83.9 %shard_map.160 = bf16[128,2048]{1,0:T(8,128)(2,1)S(1)} custom-call(bf16[2,4,8,16,2048]{4,3,2,1,0:T(8,128)(2,1)S(1)} %pad_maximum_fusion.y_ref, f32[4,8,256]{2,1,0:T(8,128)S(1)} %get-tuple-element.5.tabs_ref, bf16[128,2048]{1,0:T(8,128)(2,1)S(1)} %get-tuple-element.11.residual_ref), custom_call_target="tpu_custom_call" | custom-call | tf_op jit(solution)/shard_map/pallas_call | solution.py:333
  249.6 0.8 copy.95
  (68 shorter events, 2.4 us)
Async XLA Ops:
  0.6 3.7 %copy-start = (bf16[2048,576]{0,1:T(8,128)(2,1)S(1)}, bf16[2048,576]{0,1:T(8,128)(2,1)}, u32[]{:S(2)}) copy-start(bf16[2048,576]{0,1:T(8,128)(2,1)} %param.20) | copy-start | bytes 7077892
  6.8 8.8 %copy-start.2 = (bf16[1,128,2048]{2,1,0:T(8,128)(2,1)S(1)}, bf16[1,128,2048]{2,1,0:T(8,128)(2,1)}, u32[]{:S(2)}) copy-start(bf16[1,128,2048]{2,1,0:T(8,128)(2,1)} %param.15) | copy-start | bytes 1572868
  20.7 3.1 %copy-start.10 = (bf16[512]{0:T(512)(128)(2,1)S(1)}, bf16[512]{0:T(512)(128)(2,1)}, u32[]{:S(2)}) copy-start(bf16[512]{0:T(512)(128)(2,1)} %param.21) | copy-start | bytes 3076
  23.7 37.9 %copy-start.5 = (bf16[128,8,576]{2,0,1:T(8,128)(2,1)S(1)}, bf16[128,8,576]{2,0,1:T(8,128)(2,1)}, u32[]{:S(2)}) copy-start(bf16[128,8,576]{2,0,1:T(8,128)(2,1)} %pad_maximum_fusion.1) | copy-start | bytes 3538948
  68.9 1.9 copy-start.4
  70.9 3.2 %copy-start.6 = (bf16[8,512,128]{2,1,0:T(8,128)(2,1)S(1)}, bf16[8,512,128]{2,1,0:T(8,128)(2,1)}, u32[]{:S(2)}) copy-start(bf16[8,512,128]{2,1,0:T(8,128)(2,1)} %param.23) | copy-start | bytes 3145732
  70.9 4.1 %copy-start.3 = (bf16[1024,2048]{1,0:T(8,128)(2,1)S(1)}, bf16[1024,2048]{1,0:T(8,128)(2,1)}, u32[]{:S(2)}) copy-start(bf16[1024,2048]{1,0:T(8,128)(2,1)} %param.24) | copy-start | bytes 12582916
  75.0 1.6 copy-start.7
  75.0 1.8 copy-start.8
  75.0 1.8 copy-start.9
  133.8 6.7 %slice-start = ((s8[11534336]{0:T(1024)(128)(4,1)}), s8[3145728]{0:T(1024)(128)(4,1)S(1)}, s32[]{:S(2)}) async-start(s8[11534336]{0:T(1024)(128)(4,1)} %bitcast.112), calls=%async_computation | async-start | bytes 6291456
  134.4 6.1 %slice-start.1 = ((s8[11534336]{0:T(1024)(128)(4,1)}), s8[4194304]{0:T(1024)(128)(4,1)S(1)}, s32[]{:S(2)}) async-start(s8[11534336]{0:T(1024)(128)(4,1)} %bitcast.112), calls=%async_computation.1 | async-start | bytes 8388608
  134.4 6.1 %slice-start.2 = ((s8[11534336]{0:T(1024)(128)(4,1)}), s8[4194304]{0:T(1024)(128)(4,1)S(1)}, s32[]{:S(2)}) async-start(s8[11534336]{0:T(1024)(128)(4,1)} %bitcast.112), calls=%async_computation.2 | async-start | bytes 8388608
  165.8 84.7 %copy-start.1 = (bf16[2048,576]{0,1:T(8,128)(2,1)S(1)}, bf16[2048,576]{0,1:T(8,128)(2,1)}, u32[]{:S(2)}) copy-start(bf16[2048,576]{0,1:T(8,128)(2,1)} %param.20) | copy-start | bytes 7077892
